TPU v7x, 256 devices: a whole 4x4x8 slice. The times are simulated.
256 devices in a mesh: row: 32 (over z, y), col: 8 (over x, core).
Axes of the slice: x: 4, y: 4, z: 8, core: 2. Of those that a mesh axis runs over, the one named last changes fastest.
Arguments:
- tokens: bfloat16 [4096, 5120], P('row', 'col'), may hold values from -6 to 6
- target: bfloat16 [4096, 5120], P('row', 'col'), may hold values from -6 to 6
- w_gate: bfloat16 [5120, 13824], P('col', 'row'), may hold values from -0.078125 to 0.078125
- w_up: bfloat16 [5120, 13824], P('col', 'row'), may hold values from -0.078125 to 0.078125
- w_down: bfloat16 [13824, 5120], P('row', 'col'), may hold values from -0.0546875 to 0.0546875
- factor_u: bfloat16 [5120, 256], P('col'), may hold values from -0.078125 to 0.078125
- factor_v: bfloat16 [256, 13824], P(None, 'row'), may hold values from -3 to 3
Outputs:
- mixed: bfloat16 [4096, 5120], P('row', 'col')
- fitness: float32 [64], replicated
- update: float32 [5120, 13824], P('col', 'row')
All inputs are finite; a program needn't handle non-finite values.
Results may differ from a plain program's by a relative error of at most 0.0049.
Values may be sent and summed in bfloat16 or wider, within the bound.
No kernel may reach another device: no remote copies, remote signals or barrier semaphores. Data moves between devices by JAX's collectives and lax.ppermute only.
A program may use at most 128 MiB of HBM per device.

v0:
```python
import math
import jax
import jax.numpy as jnp
from jax import lax
from jax.sharding import PartitionSpec as P

D = 5120
RANK = 4
SEQ = 64
sigma_scale = 0.5


def apply_factors(low_three, v_three):
    return jnp.einsum("psr,prf->psf", low_three, v_three, precision=lax.Precision.HIGHEST)


def body(tokens, target, w_gate, w_up, w_down, factor_u, factor_v):
    dev_rows, dev_feat = tokens.shape
    members = factor_u.shape[1] // RANK
    units = w_up.shape[1]
    every = lax.all_gather(tokens, "row", axis=0, tiled=True)
    total_rows = every.shape[0]
    gate_part = jnp.dot(every, w_gate, preferred_element_type=jnp.float32)
    up_part = jnp.dot(every, w_up, preferred_element_type=jnp.float32)
    grouped = every.reshape(members, SEQ, dev_feat)
    u_three = factor_u.reshape(dev_feat, members, RANK)
    v_three = factor_v.reshape(members, RANK, units).astype(jnp.float32)
    low_part = jnp.einsum("psd,dpr->psr", grouped, u_three, preferred_element_type=jnp.float32)
    up_part = up_part + sigma_scale * apply_factors(low_part, v_three).reshape(total_rows, units)
    gate, up = (
        lax.psum_scatter(gate_part, "col", scatter_dimension=0, tiled=True),
        lax.psum_scatter(up_part, "col", scatter_dimension=0, tiled=True),
    )
    hidden = (jax.nn.silu(gate) * up).astype(jnp.bfloat16)
    hidden_all = lax.all_gather(hidden, "col", axis=0, tiled=True)
    out = lax.psum_scatter(
        jnp.dot(hidden_all, w_down, preferred_element_type=jnp.float32),
        "row",
        scatter_dimension=0,
        tiled=True,
    )
    mixed = out.astype(jnp.bfloat16)
    local_members = dev_rows // SEQ
    prod = (out * target.astype(jnp.float32)).reshape(local_members, SEQ * dev_feat)
    score = jnp.sum(prod, axis=1) / math.sqrt(SEQ * D)
    placed = lax.dynamic_update_slice(
        jnp.zeros((members,), jnp.float32), score, (lax.axis_index("row") * local_members,)
    )
    fitness = lax.psum(placed, ("row", "col"))
    weights = jnp.repeat(fitness, RANK)
    update = jnp.dot(
        factor_u.astype(jnp.float32) * weights[None, :],
        factor_v.astype(jnp.float32),
        precision=lax.Precision.HIGHEST,
        preferred_element_type=jnp.float32,
    ) * math.sqrt(D / members)
    return (mixed, fitness, update)


def solution(mesh):
    return jax.shard_map(
        body,
        mesh=mesh,
        in_specs=(
            P("row", "col"),
            P("row", "col"),
            P("col", "row"),
            P("col", "row"),
            P("row", "col"),
            P("col", None),
            P(None, "row"),
        ),
        out_specs=(P("row", "col"), P(), P("col", "row")),
        check_vma=False,
    )
```

profile of v0, /device:TPU:1, one launch (start us, length us, event | category | flops | bytes accessed | tf_op | source)
XLA Modules:
  0.0 587.6 jit_solution(11700659747309950121)
XLA Ops:
  7.2 0.7 all-gather.3.cloned.1.call-update
  8.0 1.2 copy.12
  9.1 0.1 reshape.22
  9.2 1.1 copy.13
  10.4 86.9 %all-gather.3.cloned.1.call-done = bf16[4096,640]{1,0:T(8,128)(2,1)} async-done(((bf16[128,640]{1,0:T(8,128)(2,1)}), bf16[4096,640]{1,0:T(8,128)(2,1)}) %all-gather.3.cloned.1.call-update) | async-done | bytes 5242896 | tf_op jit(solution)/shard_map/all_gather | solution.py:21
  97.3 4.2 fusion.4
  101.5 5.8 broadcast_multiply_fusion
  107.3 8.6 %copy.14 = f32[4096,432]{0,1:T(8,128)} copy(f32[4096,432]{1,0:T(8,128)} %bitcast.15) | data formatting | bytes 14155776 | tf_op jit(solution)/shard_map/mul | solution.py:29
  115.9 9.4 %convolution_add_fusion = f32[4096,432]{0,1:T(8,128)} fusion(f32[4096,432]{0,1:T(8,128)} %copy.14, bf16[4096,640]{1,0:T(8,128)(2,1)} %all-gather.3.cloned.1.call-done, bf16[640,432]{0,1:T(8,128)(2,1)S(1)} %copy-done.3), kind=kOutput, calls=%fused_computation | convolution fusion | flops 2266693632 | bytes 19951616 | tf_op jit(solution)/shard_map/dot_general | solution.py:24
  125.4 1.0 copy-done.6
  126.4 8.3 %fusion.3 = f32[4096,432]{0,1:T(8,128)} fusion(bf16[4096,640]{1,0:T(8,128)(2,1)} %all-gather.3.cloned.1.call-done, bf16[640,432]{0,1:T(8,128)(2,1)S(1)} %copy-done.6), kind=kOutput, calls=%fused_computation.9 | convolution fusion | flops 2264924160 | bytes 12873728 | tf_op jit(solution)/shard_map/dot_general | solution.py:23
  134.8 38.4 %reduce-scatter.6.cloned.1.call-done = f32[512,432]{0,1:T(8,128)} async-done(((f32[4096,432]{0,1:T(8,128)}), f32[512,432]{0,1:T(8,128)}) %reduce-scatter.6.cloned.1.call-update) | async-done | bytes 884752 | tf_op jit(solution)/shard_map/reduce_scatter | solution.py:32
  173.2 51.0 %reduce-scatter.4.cloned.1.call-done = f32[512,432]{0,1:T(8,128)} async-done(((f32[4096,432]{0,1:T(8,128)}), f32[512,432]{0,1:T(8,128)}) %reduce-scatter.4.cloned.1.call-update) | async-done | bytes 884752 | tf_op jit(solution)/shard_map/reduce_scatter | solution.py:31
  224.2 2.5 multiply_convert_fusion
  226.7 32.6 %all-gather.5.cloned.1.call-done = bf16[4096,432]{0,1:T(8,128)(2,1)} async-done(((bf16[512,432]{0,1:T(8,128)(2,1)}), bf16[4096,432]{0,1:T(8,128)(2,1)}) %all-gather.5.cloned.1.call-update) | async-done | bytes 3538960 | tf_op jit(solution)/shard_map/all_gather | solution.py:35
  259.3 9.5 %fusion.5 = f32[4096,640]{1,0:T(8,128)} fusion(bf16[4096,432]{0,1:T(8,128)(2,1)} %all-gather.5.cloned.1.call-done, bf16[432,640]{1,0:T(8,128)(2,1)S(1)} %copy-done), kind=kOutput, calls=%fused_computation.11 | convolution fusion | flops 2264924160 | bytes 14577664 | tf_op jit(solution)/shard_map/dot_general | solution.py:37
  268.8 229.8 %reduce-scatter.8.cloned.1.call-done = f32[128,640]{1,0:T(8,128)} async-done(((f32[4096,640]{1,0:T(8,128)}), f32[128,640]{1,0:T(8,128)}) %reduce-scatter.8.cloned.1.call-update) | async-done | bytes 327696 | tf_op jit(solution)/shard_map/reduce_scatter | solution.py:36
  498.6 1.8 multiply_reduce_fusion
  500.4 0.1 reduce_sum.14
  500.5 0.1 reduce_sum.18
  500.6 0.1 multiply_dynamic-update-slice_fusion
  500.7 78.4 %psum.7 = f32[64]{0:T(128)S(1)} all-reduce(f32[64]{0:T(128)S(1)} %multiply_dynamic-update-slice_fusion), channel_id=1, replica_groups=mesh['row'=32,'col'=8] {'row','col'}, use_global_device_ids=true, to_apply=%region_5.6 | all-reduce | flops 64 | bytes 512 | tf_op jit(solution)/shard_map/psum | solution.py:49
  579.2 0.1 mul.45
  579.3 1.8 convolution_multiply_fusion
  (25 shorter events, 0.4 us)
Async XLA Ops:
  7.2 252.2 %copy-start = (bf16[432,640]{1,0:T(8,128)(2,1)S(1)}, bf16[432,640]{1,0:T(8,128)(2,1)}, u32[]{:S(2)}) copy-start(bf16[432,640]{1,0:T(8,128)(2,1)} %param.11) | copy-start | bytes 1658884
  7.2 90.1 %all-gather.3.cloned.1.call-start = ((), (), s32[]{:S(2)}) async-start(), calls=%async_computation.3 | async-start | bytes 5406720 | tf_op jit(solution)/shard_map/all_gather | solution.py:21
  7.9 165.3 %reduce-scatter.6.cloned.1.call-start = ((), (), s32[]{:S(2)}) async-start(), calls=%async_computation.5 | async-start | bytes 7962624 | tf_op jit(solution)/shard_map/reduce_scatter | solution.py:32
  107.3 8.7 %copy-start.3 = (bf16[640,432]{0,1:T(8,128)(2,1)S(1)}, bf16[640,432]{0,1:T(8,128)(2,1)}, u32[]{:S(2)}) copy-start(bf16[640,432]{0,1:T(8,128)(2,1)} %param.10) | copy-start | bytes 1658884
  125.3 1.1 copy-start.6
  125.4 98.8 %reduce-scatter.4.cloned.1.call-start = ((), (), s32[]{:S(2)}) async-start(), calls=%async_computation.4 | async-start | bytes 7962624 | tf_op jit(solution)/shard_map/reduce_scatter | solution.py:31
  134.7 124.6 %all-gather.5.cloned.1.call-start = ((), (), s32[]{:S(2)}) async-start(), calls=%async_computation.6 | async-start | bytes 3981312 | tf_op jit(solution)/shard_map/all_gather | solution.py:35
  226.6 272.0 %reduce-scatter.8.cloned.1.call-start = ((), (), s32[]{:S(2)}) async-start(), calls=%async_computation.7 | async-start | bytes 10813440 | tf_op jit(solution)/shard_map/reduce_scatter | solution.py:36
  268.8 229.8 %copy-start.4 = (bf16[128,640]{1,0:T(8,128)(2,1)S(1)}, bf16[128,640]{1,0:T(8,128)(2,1)}, u32[]{:S(2)}) copy-start(bf16[128,640]{1,0:T(8,128)(2,1)} %param.8) | copy-start | bytes 491524
  268.8 310.5 %copy-start.1 = (bf16[640,256]{1,0:T(8,128)(2,1)S(1)}, bf16[640,256]{1,0:T(8,128)(2,1)}, u32[]{:S(2)}) copy-start(bf16[640,256]{1,0:T(8,128)(2,1)} %param.12) | copy-start | bytes 983044
  268.8 310.5 %copy-start.2 = (bf16[256,432]{0,1:T(8,128)(2,1)S(1)}, bf16[256,432]{0,1:T(8,128)(2,1)}, u32[]{:S(2)}) copy-start(bf16[256,432]{0,1:T(8,128)(2,1)} %param.13) | copy-start | bytes 663556
  579.1 2.0 copy-start.5
Sparse Core Ops, SparseCore 0:
  10.6 86.6 all-gather.2
  125.5 47.6 reduce-scatter.5
  175.8 48.3 reduce-scatter.3
  226.8 32.5 all-gather.4
  268.9 229.6 reduce-scatter.7
where the time goes:
time: 588 us
  waiting for transfers between devices  439 us (75%)
  blocking collectives  78.4 us (13%)
  matrix products  39 us (7%)
  between operations  13.8 us (2%)
  local copies, waits for them, and re-layouts  12.3 us (2%)
    reduce_scatter x1, waiting for transfers between devices, body(): lax.psum_scatter(jnp.dot(hidden_all, w_down, preferred_element_type=jnp.f...  230 us
    all_gather x1, waiting for transfers between devices, body(): every = lax.all_gather(tokens, 'row', axis=0, tiled=True)  86.9 us
    psum x1, blocking collectives, body(): fitness = lax.psum(placed, ('row', 'col'))  78.4 us
    reduce_scatter x1, waiting for transfers between devices, body(): lax.psum_scatter(gate_part, 'col', scatter_dimension=0, tiled=True)  51 us
    reduce_scatter x1, waiting for transfers between devices, body(): lax.psum_scatter(up_part, 'col', scatter_dimension=0, tiled=True)  38.4 us
    all_gather x1, waiting for transfers between devices, body(): hidden_all = lax.all_gather(hidden, 'col', axis=0, tiled=True)  32.6 us
  transfers between devices with their start and end apart: 5, of which 5 were waited for; matrix products, arithmetic and copies ran while one was open for 2% of the time, Pallas kernels for 0%

commit v1 on v0

--- a/solution.py
+++ b/solution.py
@@ -46,7 +46,7 @@
     placed = lax.dynamic_update_slice(
         jnp.zeros((members,), jnp.float32), score, (lax.axis_index("row") * local_members,)
     )
-    fitness = lax.psum(placed, ("row", "col"))
+    fitness = jnp.sum(lax.all_gather(placed, ("row", "col")), axis=0)
     weights = jnp.repeat(fitness, RANK)
     update = jnp.dot(
         factor_u.astype(jnp.float32) * weights[None, :],

time: 588 us -> 570 us (0.969)
  blocking collectives: 78.4 us -> 59.7 us
    psum x1 -> x0, blocking collectives: 78.4 us -> none  [body(): fitness = lax.psum(placed, ('row', 'col'))]
    all_gather x0 -> x1, blocking collectives: none -> 59.7 us  [body(): fitness = jnp.sum(lax.all_gather(placed, ('row', 'col')), axis=0)]
where the time goes in v1:
time: 570 us; the launch traced here: 569 us
  waiting for transfers between devices  439 us (77%)
  blocking collectives  59.7 us (10%)
  matrix products  39 us (7%)
  between operations  13.9 us (2%)
  local copies, waits for them, and re-layouts  12.5 us (2%)
    reduce_scatter x1, waiting for transfers between devices, body(): lax.psum_scatter(jnp.dot(hidden_all, w_down, preferred_element_type=jnp.f...  230 us
    all_gather x1, waiting for transfers between devices, body(): every = lax.all_gather(tokens, 'row', axis=0, tiled=True)  86.9 us
    all_gather x1, blocking collectives, body(): fitness = jnp.sum(lax.all_gather(placed, ('row', 'col')), axis=0)  59.7 us
    reduce_scatter x1, waiting for transfers between devices, body(): lax.psum_scatter(gate_part, 'col', scatter_dimension=0, tiled=True)  51 us
    reduce_scatter x1, waiting for transfers between devices, body(): lax.psum_scatter(up_part, 'col', scatter_dimension=0, tiled=True)  38.4 us
    all_gather x1, waiting for transfers between devices, body(): hidden_all = lax.all_gather(hidden, 'col', axis=0, tiled=True)  32.6 us
  transfers between devices with their start and end apart: 5, of which 5 were waited for; matrix products, arithmetic and copies ran while one was open for 2% of the time, Pallas kernels for 0%

profile of v1, /device:TPU:1, one launch (start us, length us, event | category | flops | bytes accessed | tf_op | source)
XLA Modules:
  0.0 569.3 jit_solution(11162307228326127476)
XLA Ops:
  7.2 0.7 all-gather.4.cloned.1.call-update
  8.0 1.2 copy.15
  9.2 1.1 copy.16
  10.4 86.9 %all-gather.4.cloned.1.call-done = bf16[4096,640]{1,0:T(8,128)(2,1)} async-done(((bf16[128,640]{1,0:T(8,128)(2,1)}), bf16[4096,640]{1,0:T(8,128)(2,1)}) %all-gather.4.cloned.1.call-update) | async-done | bytes 5242896 | tf_op jit(solution)/shard_map/all_gather | solution.py:21
  97.3 4.2 fusion.4
  101.5 5.8 %broadcast_multiply_fusion = f32[64,64,432]{2,1,0:T(8,128)} fusion(f32[64,64,4]{1,2,0:T(4,128)S(1)} %fusion.4, bf16[64,4,432]{2,1,0:T(4,128)(2,1)S(1)} %reshape.34), kind=kOutput, calls=%fused_computation.1 | convolution fusion | flops 86704128 | bytes 7364608 | tf_op jit(solution)/shard_map/psr,prf->psf/dot_general | solution.py:14
  107.3 8.6 %copy.17 = f32[4096,432]{0,1:T(8,128)} copy(f32[4096,432]{1,0:T(8,128)} %bitcast.17) | data formatting | bytes 14155776 | tf_op jit(solution)/shard_map/mul | solution.py:29
  115.9 9.4 %convolution_add_fusion = f32[4096,432]{0,1:T(8,128)} fusion(f32[4096,432]{0,1:T(8,128)} %copy.17, bf16[4096,640]{1,0:T(8,128)(2,1)} %all-gather.4.cloned.1.call-done, bf16[640,432]{0,1:T(8,128)(2,1)S(1)} %copy-done.3), kind=kOutput, calls=%fused_computation | convolution fusion | flops 2266693632 | bytes 19951616 | tf_op jit(solution)/shard_map/dot_general | solution.py:24
  125.4 1.0 copy-done.6
  126.4 8.3 %fusion.3 = f32[4096,432]{0,1:T(8,128)} fusion(bf16[4096,640]{1,0:T(8,128)(2,1)} %all-gather.4.cloned.1.call-done, bf16[640,432]{0,1:T(8,128)(2,1)S(1)} %copy-done.6), kind=kOutput, calls=%fused_computation.9 | convolution fusion | flops 2264924160 | bytes 12873728 | tf_op jit(solution)/shard_map/dot_general | solution.py:23
  134.8 38.4 %reduce-scatter.6.cloned.1.call-done = f32[512,432]{0,1:T(8,128)} async-done(((f32[4096,432]{0,1:T(8,128)}), f32[512,432]{0,1:T(8,128)}) %reduce-scatter.6.cloned.1.call-update) | async-done | bytes 884752 | tf_op jit(solution)/shard_map/reduce_scatter | solution.py:32
  173.2 51.0 %reduce-scatter.4.cloned.1.call-done = f32[512,432]{0,1:T(8,128)} async-done(((f32[4096,432]{0,1:T(8,128)}), f32[512,432]{0,1:T(8,128)}) %reduce-scatter.4.cloned.1.call-update) | async-done | bytes 884752 | tf_op jit(solution)/shard_map/reduce_scatter | solution.py:31
  224.2 2.5 multiply_convert_fusion
  226.7 32.6 %all-gather.6.cloned.1.call-done = bf16[4096,432]{0,1:T(8,128)(2,1)} async-done(((bf16[512,432]{0,1:T(8,128)(2,1)}), bf16[4096,432]{0,1:T(8,128)(2,1)}) %all-gather.6.cloned.1.call-update) | async-done | bytes 3538960 | tf_op jit(solution)/shard_map/all_gather | solution.py:35
  259.3 9.5 %fusion.5 = f32[4096,640]{1,0:T(8,128)} fusion(bf16[4096,432]{0,1:T(8,128)(2,1)} %all-gather.6.cloned.1.call-done, bf16[432,640]{1,0:T(8,128)(2,1)S(1)} %copy-done), kind=kOutput, calls=%fused_computation.11 | convolution fusion | flops 2264924160 | bytes 14577664 | tf_op jit(solution)/shard_map/dot_general | solution.py:37
  268.8 229.8 %reduce-scatter.8.cloned.1.call-done = f32[128,640]{1,0:T(8,128)} async-done(((f32[4096,640]{1,0:T(8,128)}), f32[128,640]{1,0:T(8,128)}) %reduce-scatter.8.cloned.1.call-update) | async-done | bytes 327696 | tf_op jit(solution)/shard_map/reduce_scatter | solution.py:36
  498.6 1.8 multiply_reduce_fusion
  500.4 0.1 reduce_sum.26
  500.5 0.1 reduce_sum.27
  500.6 0.1 dynamic_update_slice.5
  500.8 59.7 %all-gather = f32[256,1,64]{2,1,0:T(1,128)S(1)} all-gather(f32[1,1,64]{2,1,0:T(1,128)S(1)} %dynamic_update_slice.5), channel_id=1, replica_groups=mesh['row'=32,'col'=8] {'row','col'}, dimensions={0}, use_global_device_ids=true | all-gather | bytes 65792 | tf_op jit(solution)/shard_map/all_gather | solution.py:49
  560.5 0.3 reduce_sum.28
  560.8 0.1 mul.45
  561.0 1.8 convolution_multiply_fusion
  (27 shorter events, 0.5 us)
Async XLA Ops:
  7.2 252.2 %copy-start = (bf16[432,640]{1,0:T(8,128)(2,1)S(1)}, bf16[432,640]{1,0:T(8,128)(2,1)}, u32[]{:S(2)}) copy-start(bf16[432,640]{1,0:T(8,128)(2,1)} %param.11) | copy-start | bytes 1658884
  7.2 90.1 %all-gather.4.cloned.1.call-start = ((), (), s32[]{:S(2)}) async-start(), calls=%async_computation.3 | async-start | bytes 5406720 | tf_op jit(solution)/shard_map/all_gather | solution.py:21
  7.9 165.3 %reduce-scatter.6.cloned.1.call-start = ((), (), s32[]{:S(2)}) async-start(), calls=%async_computation.5 | async-start | bytes 7962624 | tf_op jit(solution)/shard_map/reduce_scatter | solution.py:32
  107.3 8.7 %copy-start.3 = (bf16[640,432]{0,1:T(8,128)(2,1)S(1)}, bf16[640,432]{0,1:T(8,128)(2,1)}, u32[]{:S(2)}) copy-start(bf16[640,432]{0,1:T(8,128)(2,1)} %param.10) | copy-start | bytes 1658884
  125.3 1.1 copy-start.6
  125.4 98.8 %reduce-scatter.4.cloned.1.call-start = ((), (), s32[]{:S(2)}) async-start(), calls=%async_computation.4 | async-start | bytes 7962624 | tf_op jit(solution)/shard_map/reduce_scatter | solution.py:31
  134.7 124.6 %all-gather.6.cloned.1.call-start = ((), (), s32[]{:S(2)}) async-start(), calls=%async_computation.6 | async-start | bytes 3981312 | tf_op jit(solution)/shard_map/all_gather | solution.py:35
  226.6 272.0 %reduce-scatter.8.cloned.1.call-start = ((), (), s32[]{:S(2)}) async-start(), calls=%async_computation.7 | async-start | bytes 10813440 | tf_op jit(solution)/shard_map/reduce_scatter | solution.py:36
  268.8 229.8 %copy-start.4 = (bf16[128,640]{1,0:T(8,128)(2,1)S(1)}, bf16[128,640]{1,0:T(8,128)(2,1)}, u32[]{:S(2)}) copy-start(bf16[128,640]{1,0:T(8,128)(2,1)} %param.8) | copy-start | bytes 491524
  268.8 292.2 %copy-start.1 = (bf16[640,256]{1,0:T(8,128)(2,1)S(1)}, bf16[640,256]{1,0:T(8,128)(2,1)}, u32[]{:S(2)}) copy-start(bf16[640,256]{1,0:T(8,128)(2,1)} %param.12) | copy-start | bytes 983044
  268.8 292.2 %copy-start.2 = (bf16[256,432]{0,1:T(8,128)(2,1)S(1)}, bf16[256,432]{0,1:T(8,128)(2,1)}, u32[]{:S(2)}) copy-start(bf16[256,432]{0,1:T(8,128)(2,1)} %param.13) | copy-start | bytes 663556
  560.8 2.0 copy-start.5
Sparse Core Ops, SparseCore 0:
  10.6 86.6 all-gather.3
  125.5 47.6 reduce-scatter.5
  175.8 48.3 reduce-scatter.3
  226.8 32.5 all-gather.5
  268.9 229.6 reduce-scatter.7
